TPU v7x, 32 devices: a whole 2x2x4 slice. The times are simulated.
32 devices in a mesh: dp: 4 (over y, x), tensor: 8 (over z, core).
Axes of the slice: x: 2, y: 2, z: 4, core: 2. Of those that a mesh axis runs over, the one named last changes fastest.
Arguments:
- acts: bfloat16 [32, 512, 28672], P('dp', None, 'tensor'), may hold values from -6 to 6
- grads: bfloat16 [32, 512, 8192], P('dp', None, 'tensor'), may hold values from -6 to 6
- proj_in: bfloat16 [28672, 64], P('tensor'), may hold values from -0.03125 to 0.03125
- proj_out: bfloat16 [8192, 64], P('tensor'), may hold values from -0.0625 to 0.0625
- queries: float32 [256, 4096], P('dp', 'tensor'), may hold values from -6 to 6
Outputs:
- scores: float32 [32, 256], P('dp')
All inputs are finite; a program needn't handle non-finite values.
Results may differ from a plain program's by a relative error of at most 0.0003.
Values sent between devices are 32-bit elements; how exact they have to be, the bound alone decides.
A program may use at most 128 MiB of HBM per device.

v0:
```python
import jax
import jax.numpy as jnp
from jax import lax
from jax.sharding import PartitionSpec as P


def score_block(encoded, n_query):

    def add_block(carry, piece, start):
        block = jnp.einsum("ek,qk->eq", encoded, piece, precision=lax.Precision.HIGHEST)
        return block

    empty = jnp.zeros((encoded.shape[0], n_query), jnp.float32)
    return (add_block, empty)


def per_device(acts, grads, proj_in, proj_out, queries):
    examples, length, width_in = acts.shape
    width_out = grads.shape[2]
    rank = proj_in.shape[1]
    n_query = queries.shape[0] * lax.axis_size("dp")
    partial_in = jnp.dot(
        acts.reshape(examples * length, width_in), proj_in, preferred_element_type=jnp.float32
    )
    partial_out = jnp.dot(
        grads.reshape(examples * length, width_out), proj_out, preferred_element_type=jnp.float32
    )
    factor = length ** (-0.5)
    side_in, side_out = lax.psum((partial_in, partial_out), "tensor")
    encoded = jnp.einsum(
        "eti,etj->eij",
        side_out.reshape(examples, length, rank),
        side_in.reshape(examples, length, rank),
        precision=lax.Precision.HIGHEST,
    )
    encoded = (encoded * factor).reshape(examples, rank * rank)
    wide_queries = lax.all_gather(queries, "tensor", axis=1, tiled=True)
    add_block, empty = score_block(encoded, n_query)
    total = add_block(empty, lax.all_gather(wide_queries, "dp", axis=0, tiled=True), jnp.int32(0))
    return total / rank


def solution(mesh):
    in_specs = (
        P("dp", None, "tensor"),
        P("dp", None, "tensor"),
        P("tensor", None),
        P("tensor", None),
        P("dp", "tensor"),
    )
    out_specs = P("dp", None)
    return jax.shard_map(
        per_device, mesh=mesh, in_specs=in_specs, out_specs=out_specs, check_vma=False
    )
```

profile of v0, /device:TPU:0, one launch (start us, length us, event | category | flops | bytes accessed | tf_op | source)
XLA Modules:
  0.0 167.7 jit_solution(13488403836978778373)
XLA Ops:
  6.5 0.0 copy-start
  6.5 0.0 all-gather.3.cloned.1.call-start
  6.5 0.7 all-gather.3.cloned.1.call-update
  7.3 0.0 all-reduce.3.cloned.1.call-start
  7.3 6.0 %fusion = f32[4096,64]{0,1:T(8,128)S(1)} fusion(bf16[4096,1024]{1,0:T(8,128)(2,1)} %bitcast.17, bf16[1024,64]{0,1:T(8,128)(2,1)} %param.8), kind=kOutput, calls=%fused_computation.4 | convolution fusion | flops 536870912 | bytes 9568256 | tf_op jit(solution)/shard_map/dot_general | solution.py:25
  13.3 0.0 copy-done
  13.4 14.2 %fusion.1 = f32[4096,64]{0,1:T(8,128)S(1)} fusion(bf16[4096,3584]{1,0:T(8,128)(2,1)} %bitcast.16, bf16[3584,64]{0,1:T(8,128)(2,1)S(1)} %copy-done), kind=kOutput, calls=%fused_computation.5 | convolution fusion | flops 1879048192 | bytes 30867456 | tf_op jit(solution)/shard_map/dot_general | solution.py:22
  27.6 1.6 copy_bitcast_fusion
  29.2 0.0 all-reduce.3.cloned.1.call-update
  29.2 0.0 all-gather.5.cloned.1.call-start
  29.3 4.5 %all-gather.3.cloned.1.call-done = f32[64,4096]{1,0:T(8,128)} async-done(((f32[64,512]{1,0:T(8,128)}), f32[64,4096]{1,0:T(8,128)}) %all-gather.3.cloned.1.call-update) | async-done | bytes 1048592 | tf_op jit(solution)/shard_map/all_gather | solution.py:37
  33.8 0.0 all-gather.5.cloned.1.call-update
  33.8 66.9 %all-reduce.3.cloned.1.call-done = (f32[8,512,64]{1,2,0:T(8,128)}, f32[8,512,64]{1,2,0:T(8,128)}) async-done(((f32[8,512,64]{1,2,0:T(8,128)}, f32[8,512,64]{1,2,0:T(8,128)}), (f32[8,512,64]{1,2,0:T(8,128)}, f32[8,512,64]{1,2,0:T(8,128)})) %all-reduce.3.cloned.1.call-update) | async-done | bytes 2097168 | tf_op jit(solution)/shard_map/psum | solution.py:29
  100.8 2.6 %convolution_multiply_fusion = f32[8,64,64]{2,1,0:T(8,128)S(1)} fusion(f32[8,512,64]{1,2,0:T(8,128)} %get-tuple-element.5, f32[8,512,64]{1,2,0:T(8,128)} %get-tuple-element.6), kind=kOutput, calls=%fused_computation | convolution fusion | flops 201359360 | bytes 2228224 | tf_op jit(solution)/shard_map/eti,etj->eij/dot_general | solution.py:30
  103.4 0.1 reshape.19
  103.5 51.5 %all-gather.5.cloned.1.call-done = f32[256,4096]{1,0:T(8,128)} async-done(((f32[64,4096]{1,0:T(8,128)}), f32[256,4096]{1,0:T(8,128)}) %all-gather.5.cloned.1.call-update) | async-done | bytes 4194320 | tf_op jit(solution)/shard_map/all_gather | solution.py:39
  155.0 6.1 %convolution_multiply_fusion.1 = f32[8,256]{1,0:T(8,128)} fusion(f32[8,4096]{1,0:T(8,128)S(1)} %reshape.19, f32[256,4096]{1,0:T(8,128)} %all-gather.5.cloned.1.call-done), kind=kOutput, calls=%fused_computation.1 | convolution fusion | flops 100665344 | bytes 4333568 | tf_op jit(solution)/shard_map/ek,qk->eq/dot_general | solution.py:10
Async XLA Ops:
  6.5 6.8 %copy-start = (bf16[3584,64]{0,1:T(8,128)(2,1)S(1)}, bf16[3584,64]{0,1:T(8,128)(2,1)}, u32[]{:S(2)}) copy-start(bf16[3584,64]{0,1:T(8,128)(2,1)} %param.7) | copy-start | bytes 1376260
  6.5 27.3 %all-gather.3.cloned.1.call-start = ((), (), s32[]{:S(2)}) async-start(), calls=%async_computation | async-start | bytes 1179648 | tf_op jit(solution)/shard_map/all_gather | solution.py:37
  7.3 93.5 %all-reduce.3.cloned.1.call-start = ((), (), s32[]{:S(2)}) async-start(), calls=%async_computation.2 | async-start | bytes 4194304 | tf_op jit(solution)/shard_map/psum | solution.py:29
  29.2 125.8 %all-gather.5.cloned.1.call-start = ((), (), s32[]{:S(2)}) async-start(), calls=%async_computation.1 | async-start | bytes 5242880 | tf_op jit(solution)/shard_map/all_gather | solution.py:39
Sparse Core Ops, SparseCore 0:
  9.0 24.7 all-gather.2
  36.2 64.5 all-reduce.2
  102.6 52.3 all-gather.4
where the time goes:
time: 168 us
  waiting for transfers between devices  124 us (74%)
  matrix products  29 us (17%)
  between operations  13.1 us (8%)
  local copies, waits for them, and re-layouts  1.74 us (1%)
    psum x1, waiting for transfers between devices, per_device(): side_in, side_out = lax.psum((partial_in, partial_out), 'tensor')  66.9 us
    all_gather x1, waiting for transfers between devices, per_device(): lax.all_gather(wide_queries, 'dp', axis=0, tiled=True)  51.5 us
    dot_general x1, matrix products, per_device(): jnp.dot(acts.reshape(examples * length, width_in), proj_in, preferred_ele...  14.2 us
    dot_general x1, matrix products, add_block(): jnp.einsum('ek,qk->eq', encoded, piece, precision=lax.Precision.HIGHEST)  6.14 us
    dot_general x1, matrix products, per_device(): jnp.dot(grads.reshape(examples * length, width_out), proj_out, preferred_...  6.04 us
    all_gather x1, waiting for transfers between devices, per_device(): wide_queries = lax.all_gather(queries, 'tensor', axis=1, tiled=True)  4.52 us
  transfers between devices with their start and end apart: 3, of which 3 were waited for; matrix products, arithmetic and copies ran while one was open for 15% of the time, Pallas kernels for 0%

commit v1 on v0

v1 whole, which is shorter than its diff:
```python
import functools

import jax
import jax.numpy as jnp
from jax import lax
from jax.experimental import pallas as pl
from jax.experimental.pallas import tpu as pltpu
from jax.sharding import PartitionSpec as P

MESH = pl.DeviceIdType.MESH
CHUNK = 128
SLOTS = 4


def kernel(n_dp, n_tensor, acts, grads, proj_in, proj_out, queries, out,
           x, x_sem, w_in, w_out, w, w_sem,
           part, pair, pair_send, pair_recv, chain, chain_send, chain_recv,
           gram, enc, enc_send, enc_recv,
           q_all, q_own_sem, q_send, q_recv,
           score, score_send, score_recv):
    examples, length, width_in = acts.shape
    width = x.shape[2]
    rank = proj_in.shape[1]
    blocks = length // CHUNK
    each = examples // 4
    items = each * blocks
    line = n_tensor // 2

    me = lax.axis_index("tensor")
    me_dp = lax.axis_index("dp")
    place = me // 2
    core = me % 2
    sibling = me + 1 - 2 * core
    is_end = jnp.logical_or(place == 0, place == line - 1)
    near = jnp.where(place < line // 2, 1, 0)
    near_hops = jnp.where(near == 1, place, line - 1 - place)
    far_hops = line - 1 - near_hops

    def where_is(s, u):
        half = items // 2
        late = s // half
        direction = jnp.where(is_end, near + late - 2 * near * late, u)
        item = jnp.where(is_end, 2 * (s % half) + u, s)
        return direction, item

    def start_load(s):
        slot = s % SLOTS
        for u in range(2):
            direction, item = where_is(s, u)
            start = pl.multiple_of((item % blocks) * CHUNK, CHUNK)
            for owner in range(2):
                e = (direction * 2 + owner) * each + item // blocks
                rows = pl.ds((2 * u + owner) * CHUNK, CHUNK)
                pltpu.make_async_copy(
                    acts.at[e, pl.ds(start, CHUNK), :],
                    x.at[slot, rows, pl.ds(0, width_in)], x_sem.at[slot]).start()
                pltpu.make_async_copy(
                    grads.at[e, pl.ds(start, CHUNK), :],
                    x.at[slot, rows, pl.ds(width_in, width - width_in)], x_sem.at[slot]).start()

    barrier = pltpu.get_barrier_semaphore()
    for r in range(1, n_tensor):
        pl.semaphore_signal(barrier, inc=1, device_id={"tensor": (me + r) % n_tensor}, device_id_type=MESH)
    for r in range(1, n_dp):
        pl.semaphore_signal(barrier, inc=1, device_id={"dp": (me_dp + r) % n_dp}, device_id_type=MESH)

    load_in = pltpu.make_async_copy(proj_in, w_in, w_sem.at[0])
    load_out = pltpu.make_async_copy(proj_out, w_out, w_sem.at[1])
    load_in.start()
    load_out.start()
    for s in range(SLOTS - 1):
        start_load(s)
    q_own = pltpu.make_async_copy(queries, q_all.at[me_dp], q_own_sem)
    q_own.start()
    load_in.wait()
    load_out.wait()
    w[pl.ds(0, width_in), :] = jnp.concatenate([w_in[...], jnp.zeros_like(w_in)], axis=1)
    w[pl.ds(width_in, width - width_in), :] = jnp.concatenate([jnp.zeros_like(w_out), w_out[...]], axis=1)

    pl.semaphore_wait(barrier, n_tensor + n_dp - 2)

    def query_copy(r):
        return pltpu.make_async_remote_copy(
            src_ref=queries, dst_ref=q_all.at[me_dp], send_sem=q_send.at[r - 1], recv_sem=q_recv.at[r - 1],
            device_id={"dp": (me_dp + r) % n_dp}, device_id_type=MESH)

    for r in range(1, n_dp):
        query_copy(r).start()

    def pair_copy(direction, item):
        return pltpu.make_async_remote_copy(
            src_ref=part.at[direction, item, 1 - core], dst_ref=pair.at[direction, item],
            send_sem=pair_send.at[direction, item], recv_sem=pair_recv.at[direction, item],
            device_id={"tensor": sibling}, device_id_type=MESH)

    def chain_copy(direction, item):
        return pltpu.make_async_remote_copy(
            src_ref=part.at[direction, item, core], dst_ref=chain.at[direction, item],
            send_sem=chain_send.at[direction, item], recv_sem=chain_recv.at[direction, item],
            device_id={"tensor": (me + 4 * direction - 2 + n_tensor) % n_tensor}, device_id_type=MESH)

    group = enc.shape[1]

    def enc_rows(t):
        return pl.ds(pl.multiple_of((rank + t * rank // n_tensor) // group * group, group), group)

    def enc_copy(j, e, r):
        to = (me + r) % n_tensor
        return pltpu.make_async_remote_copy(
            src_ref=gram.at[j, enc_rows(to), :], dst_ref=enc.at[e],
            send_sem=enc_send.at[j, r - 1], recv_sem=enc_recv.at[e],
            device_id={"tensor": to}, device_id_type=MESH)

    def process(direction, item, hops):
        pair_copy(direction, item).wait_recv()
        part[direction, item, core] = part[direction, item, core] + pair[direction, item]

        @pl.when(hops > 0)
        def _():
            chain_copy(direction, item).wait_recv()
            part[direction, item, core] = part[direction, item, core] + chain[direction, item]

        @pl.when(hops < line - 1)
        def _():
            chain_copy(direction, item).start()

        @pl.when(hops == line - 1)
        def _():
            side = part[direction, item, core]
            j = item // blocks
            e = (direction * 2 + core) * each + j
            add = lax.dot_general(side, side, (((0,), (0,)), ((), ())),
                                  precision=lax.Precision.HIGHEST, preferred_element_type=jnp.float32)

            @pl.when(item % blocks == 0)
            def _():
                gram[j] = add

            @pl.when(item % blocks != 0)
            def _():
                gram[j] = gram[j] + add

            @pl.when(item % blocks == blocks - 1)
            def _():
                for r in range(1, n_tensor):
                    enc_copy(j, e, r).start()
                enc[e] = gram[j, enc_rows(me), :]

    def step(s, carry):
        @pl.when(s < items)
        def _():
            slot = s % SLOTS

            @pl.when(s + SLOTS - 1 < items)
            def _():
                start_load(s + SLOTS - 1)

            pltpu.make_async_copy(x.at[slot], x.at[slot], x_sem.at[slot]).wait()
            sides = jnp.dot(x[slot], w[...], preferred_element_type=jnp.float32)
            for u in range(2):
                direction, item = where_is(s, u)
                for owner in range(2):
                    part[direction, item, owner] = sides[(2 * u + owner) * CHUNK:(2 * u + owner + 1) * CHUNK]
                pair_copy(direction, item).start()

        first = jnp.where(is_end, 2 * (s - 1), s - 1 - 2 * near_hops)
        count = jnp.where(is_end, 2, 1)
        for u in range(2):
            item = first + u

            @pl.when(jnp.logical_and(u < count, jnp.logical_and(item >= 0, item < items)))
            def _():
                process(near, item, near_hops)

        item_far = s - 1 - 2 * far_hops

        @pl.when(jnp.logical_and(item_far >= 0, item_far < items))
        def _():
            process(1 - near, item_far, far_hops)

        return carry

    lax.fori_loop(0, items + 2 * (line - 1) + 1, step, 0)

    q_own.wait()
    for r in range(1, n_dp):
        query_copy(r).wait_recv()
    for e in range(examples):
        owner = (0 if e < examples // 2 else n_tensor - 2) + (e // each) % 2

        @pl.when(me != owner)
        def _():
            enc_copy(0, e, 1).wait_recv()

    per = rank // n_tensor
    lane = lax.broadcasted_iota(jnp.int32, (examples, 2 * rank), 1)
    shift = me * per % group // per
    total = None
    for m in range(per // 2):
        picked = None
        for v in range(group // per):
            low = enc[:, v * per + 2 * m, :]
            high = enc[:, v * per + 2 * m + 1, :]
            both = jnp.where(lane < rank, low, pltpu.roll(high, rank, 1))
            picked = both if picked is None else jnp.where(shift == v, both, picked)
        rows = q_all[:, :, pl.ds(2 * rank * m, 2 * rank)].reshape(-1, 2 * rank)
        add = lax.dot_general(picked, rows, (((1,), (1,)), ((), ())),
                              precision=lax.Precision.HIGHEST, preferred_element_type=jnp.float32)
        total = add if total is None else total + add
    score[me] = total

    def score_copy(r):
        return pltpu.make_async_remote_copy(
            src_ref=score.at[me], dst_ref=score.at[me],
            send_sem=score_send.at[r - 1], recv_sem=score_recv.at[r - 1],
            device_id={"tensor": (me + r) % n_tensor}, device_id_type=MESH)

    def score_arrival(r):
        frm = (me - r + n_tensor) % n_tensor
        return pltpu.make_async_remote_copy(
            src_ref=score.at[frm], dst_ref=score.at[frm],
            send_sem=score_send.at[r - 1], recv_sem=score_recv.at[r - 1],
            device_id={"tensor": (me + r) % n_tensor}, device_id_type=MESH)

    for r in range(1, n_tensor):
        score_copy(r).start()
    for r in range(1, n_tensor):
        score_arrival(r).wait_recv()
    result = score[0]
    for t in range(1, n_tensor):
        result = result + score[t]
    out[...] = result * (length ** (-0.5) / rank)

    for r in range(1, n_tensor):
        score_copy(r).wait_send()
    for r in range(1, n_dp):
        query_copy(r).wait_send()

    def drain(i, carry):
        for direction in range(2):
            pair_copy(direction, i).wait_send()
            hops = jnp.where(near == direction, near_hops, far_hops)

            @pl.when(hops < line - 1)
            def _():
                chain_copy(direction, i).wait_send()

        return carry

    lax.fori_loop(0, items, drain, 0)

    @pl.when(is_end)
    def _():
        for j in range(each):
            for r in range(1, n_tensor):
                enc_copy(j, 0, r).wait_send()


def per_device(acts, grads, proj_in, proj_out, queries):
    examples, length, width_in = acts.shape
    width_out = grads.shape[2]
    rank = proj_in.shape[1]
    n_dp, n_tensor = lax.axis_size("dp"), lax.axis_size("tensor")
    n_query = queries.shape[0] * n_dp
    items = examples // 4 * (length // CHUNK)
    width = width_in + width_out
    group = max(rank // n_tensor, 8)
    f32, bf16, dma = jnp.float32, jnp.bfloat16, pltpu.SemaphoreType.DMA
    anywhere = pl.BlockSpec(memory_space=pl.ANY)
    tokens = examples * length
    return pl.pallas_call(
        functools.partial(kernel, n_dp, n_tensor),
        out_shape=jax.ShapeDtypeStruct((examples, n_query), f32),
        in_specs=[anywhere] * 5,
        out_specs=pl.BlockSpec(memory_space=pltpu.VMEM),
        scratch_shapes=[
            pltpu.VMEM((SLOTS, 4 * CHUNK, width), bf16), dma((SLOTS,)),
            pltpu.VMEM((width_in, rank), bf16), pltpu.VMEM((width_out, rank), bf16),
            pltpu.VMEM((width, 2 * rank), bf16), dma((2,)),
            pltpu.VMEM((2, items, 2, CHUNK, 2 * rank), f32),
            pltpu.VMEM((2, items, CHUNK, 2 * rank), f32), dma((2, items)), dma((2, items)),
            pltpu.VMEM((2, items, CHUNK, 2 * rank), f32), dma((2, items)), dma((2, items)),
            pltpu.VMEM((examples // 4, 2 * rank, 2 * rank), f32),
            pltpu.VMEM((examples, group, 2 * rank), f32),
            dma((examples // 4, n_tensor - 1)), dma((examples,)),
            pltpu.VMEM((n_dp,) + queries.shape, f32), dma(()), dma((n_dp - 1,)), dma((n_dp - 1,)),
            pltpu.VMEM((n_tensor, examples, n_query), f32), dma((n_tensor - 1,)), dma((n_tensor - 1,)),
        ],
        compiler_params=pltpu.CompilerParams(
            collective_id=0, has_side_effects=True, vmem_limit_bytes=48 * 1024 * 1024),
        cost_estimate=pl.CostEstimate(
            flops=2 * tokens * width * rank, bytes_accessed=2 * tokens * width, transcendentals=0),
    )(acts, grads, proj_in, proj_out, queries)


def solution(mesh):
    in_specs = (
        P("dp", None, "tensor"),
        P("dp", None, "tensor"),
        P("tensor", None),
        P("tensor", None),
        P("dp", "tensor"),
    )
    out_specs = P("dp", None)
    return jax.shard_map(
        per_device, mesh=mesh, in_specs=in_specs, out_specs=out_specs, check_vma=False
    )
```

time: 168 us -> 42.7 us (0.25)
  waiting for transfers between devices: 124 us -> 0 us
  Pallas kernels: 0 us -> 38.4 us
  matrix products: 29 us -> 0 us
  between operations: 13.1 us -> 0.03 us
  local copies, waits for them, and re-layouts: 1.74 us -> 4.02 us
    psum x1 -> x0, waiting for transfers between devices: 66.9 us -> none  [per_device(): side_in, side_out = lax.psum((partial_in, partial_out), 'tensor')]
    all_gather x2 -> x0, waiting for transfers between devices: 56 us -> none  [the longest x1 51.5 us: per_device(): lax.all_gather(wide_queries, 'dp', axis=0, tiled=True)]
    pallas_call x0 -> x1, Pallas kernels: none -> 38.4 us  [per_device(): pl.pallas_call(functools.partial(kernel, n_dp, n_tensor), out_shape=jax.S...]
    dot_general x4 -> x0, matrix products: 29 us -> none  [the longest x1 14.2 us: per_device(): jnp.dot(acts.reshape(examples * length, width_in), proj_in, preferred_ele...]
    unnamed x2 -> x5, local copies, waits for them, and re-layouts: 0.01 us -> 4.02 us
    reshape x2 -> x0, local copies, waits for them, and re-layouts: 1.74 us -> none  [the longest x1 1.62 us: per_device(): side_in.reshape(examples, length, rank)]
  transfers between devices with their start and end apart: 3 -> 0, of which waited for: 3 -> 0; matrix products, arithmetic and copies ran while one was open for 15% -> 0% of each run, Pallas kernels for 0% -> 0%
where the time goes in v1:
time: 42.7 us; the launch traced here: 42.5 us
  Pallas kernels  38.4 us (90%)
  local copies, waits for them, and re-layouts  4.02 us (9%)
    pallas_call x1, Pallas kernels, per_device(): pl.pallas_call(functools.partial(kernel, n_dp, n_tensor), out_shape=jax.S...  38.4 us
    unnamed x5, local copies, waits for them, and re-layouts  4.02 us

profile of v1, /device:TPU:0, one launch (start us, length us, event | category | flops | bytes accessed | tf_op | source)
XLA Modules:
  0.0 42.5 jit_solution(7084026832198868749)
XLA Ops:
  0.0 1.1 %copy.7.proj_out = bf16[1024,64]{1,0:T(8,128)(2,1)S(1)} copy(bf16[1024,64]{0,1:T(8,128)(2,1)} %param.8) | data formatting | bytes 262144 | tf_op args[3]
  1.1 1.4 %copy.6.proj_in = bf16[3584,64]{1,0:T(8,128)(2,1)S(1)} copy(bf16[3584,64]{0,1:T(8,128)(2,1)} %param.7) | data formatting | bytes 917504 | tf_op args[2]
  2.5 0.0 copy-start
  2.5 0.9 %copy-done = f32[64,512]{1,0:T(8,128)S(1)} copy-done((f32[64,512]{1,0:T(8,128)S(1)}, f32[64,512]{1,0:T(8,128)}, u32[]{:S(2)}) %copy-start) | copy-done | bytes 131096
  3.4 38.4 %shard_map.55 = f32[8,256]{1,0:T(8,128)S(1)} custom-call(bf16[8,512,3584]{2,1,0:T(8,128)(2,1)} %acts.1, bf16[8,512,1024]{2,1,0:T(8,128)(2,1)} %grads.1, bf16[3584,64]{1,0:T(8,128)(2,1)S(1)} %copy.6.proj_in, bf16[1024,64]{1,0:T(8,128)(2,1)S(1)} %copy.7.proj_out, f32[64,512]{1,0:T(8,128)S(1)} %copy-done), custom_call_target="tpu_custom_call" | custom-call | flops 2415919104 | bytes 37748736 | tf_op jit(solution)/shard_map/pallas_call | solution.py:271
  41.9 0.6 %copy.9 = f32[8,256]{1,0:T(8,128)} copy(f32[8,256]{1,0:T(8,128)S(1)} %shard_map.55) | data formatting | bytes 16384
Async XLA Ops:
  2.5 0.9 %copy-start = (f32[64,512]{1,0:T(8,128)S(1)}, f32[64,512]{1,0:T(8,128)}, u32[]{:S(2)}) copy-start(f32[64,512]{1,0:T(8,128)} %queries.1) | copy-start | bytes 393220

commit v2 on v1

--- a/solution.py
+++ b/solution.py
@@ -8,19 +8,30 @@
 from jax.sharding import PartitionSpec as P
 
 MESH = pl.DeviceIdType.MESH
-CHUNK = 128
-SLOTS = 4
+CHUNK = 64
+SLOTS = 5
+BASE = 2
+LAG = 3
+
+
+def split(value):
+    high = value.astype(jnp.bfloat16)
+    return high, (value - high.astype(jnp.float32)).astype(jnp.bfloat16)
+
+
+def dot(a, b, over):
+    return lax.dot_general(a, b, ((over[:1], over[1:]), ((), ())), preferred_element_type=jnp.float32)
 
 
 def kernel(n_dp, n_tensor, acts, grads, proj_in, proj_out, queries, out,
-           x, x_sem, w_in, w_out, w, w_sem,
+           x, x_sem, w_side, w, w_sem,
            part, pair, pair_send, pair_recv, chain, chain_send, chain_recv,
            gram, enc, enc_send, enc_recv,
-           q_all, q_own_sem, q_send, q_recv,
+           q_all, q_high, q_low, q_own_sem, q_send, q_recv,
            score, score_send, score_recv):
     examples, length, width_in = acts.shape
     width = x.shape[2]
-    rank = proj_in.shape[1]
+    rank = proj_in.shape[0]
     blocks = length // CHUNK
     each = examples // 4
     items = each * blocks
@@ -64,28 +75,26 @@
     for r in range(1, n_dp):
         pl.semaphore_signal(barrier, inc=1, device_id={"dp": (me_dp + r) % n_dp}, device_id_type=MESH)
 
-    load_in = pltpu.make_async_copy(proj_in, w_in, w_sem.at[0])
-    load_out = pltpu.make_async_copy(proj_out, w_out, w_sem.at[1])
+    in_lanes, out_lanes = pl.ds(0, width_in), pl.ds(width_in, width - width_in)
+    in_rows, out_rows = pl.ds(0, rank), pl.ds(rank, rank)
+    load_in = pltpu.make_async_copy(proj_in, w_side.at[in_rows, in_lanes], w_sem.at[0])
+    load_out = pltpu.make_async_copy(proj_out, w_side.at[out_rows, out_lanes], w_sem.at[1])
     load_in.start()
     load_out.start()
     for s in range(SLOTS - 1):
         start_load(s)
     q_own = pltpu.make_async_copy(queries, q_all.at[me_dp], q_own_sem)
     q_own.start()
+    w_side[out_rows, in_lanes] = jnp.zeros((rank, width_in), w_side.dtype)
+    w_side[in_rows, out_lanes] = jnp.zeros((rank, width - width_in), w_side.dtype)
     load_in.wait()
     load_out.wait()
-    w[pl.ds(0, width_in), :] = jnp.concatenate([w_in[...], jnp.zeros_like(w_in)], axis=1)
-    w[pl.ds(width_in, width - width_in), :] = jnp.concatenate([jnp.zeros_like(w_out), w_out[...]], axis=1)
-
-    pl.semaphore_wait(barrier, n_tensor + n_dp - 2)
+    w[...] = w_side[...].T
 
     def query_copy(r):
         return pltpu.make_async_remote_copy(
             src_ref=queries, dst_ref=q_all.at[me_dp], send_sem=q_send.at[r - 1], recv_sem=q_recv.at[r - 1],
             device_id={"dp": (me_dp + r) % n_dp}, device_id_type=MESH)
-
-    for r in range(1, n_dp):
-        query_copy(r).start()
 
     def pair_copy(direction, item):
         return pltpu.make_async_remote_copy(
@@ -129,8 +138,8 @@
             side = part[direction, item, core]
             j = item // blocks
             e = (direction * 2 + core) * each + j
-            add = lax.dot_general(side, side, (((0,), (0,)), ((), ())),
-                                  precision=lax.Precision.HIGHEST, preferred_element_type=jnp.float32)
+            high, low = split(side)
+            add = dot(jnp.concatenate([high, high, low], axis=0), jnp.concatenate([high, low, high], axis=0), (0, 0))
 
             @pl.when(item % blocks == 0)
             def _():
@@ -161,9 +170,27 @@
                 direction, item = where_is(s, u)
                 for owner in range(2):
                     part[direction, item, owner] = sides[(2 * u + owner) * CHUNK:(2 * u + owner + 1) * CHUNK]
+
+            @pl.when(s == 0)
+            def _():
+                pl.semaphore_wait(barrier, n_tensor + n_dp - 2)
+                for r in range(1, n_dp):
+                    query_copy(r).start()
+
+            for u in range(2):
+                direction, item = where_is(s, u)
                 pair_copy(direction, item).start()
 
-        first = jnp.where(is_end, 2 * (s - 1), s - 1 - 2 * near_hops)
+        @pl.when(s == items)
+        def _():
+            q_own.wait()
+            for r in range(1, n_dp):
+                query_copy(r).wait_recv()
+            high, low = split(q_all[...].reshape(q_high.shape))
+            q_high[...] = high
+            q_low[...] = low
+
+        first = jnp.where(is_end, 2 * (s - BASE), s - BASE - LAG * near_hops)
         count = jnp.where(is_end, 2, 1)
         for u in range(2):
             item = first + u
@@ -172,7 +199,7 @@
             def _():
                 process(near, item, near_hops)
 
-        item_far = s - 1 - 2 * far_hops
+        item_far = s - BASE - LAG * far_hops
 
         @pl.when(jnp.logical_and(item_far >= 0, item_far < items))
         def _():
@@ -180,11 +207,8 @@
 
         return carry
 
-    lax.fori_loop(0, items + 2 * (line - 1) + 1, step, 0)
-
-    q_own.wait()
-    for r in range(1, n_dp):
-        query_copy(r).wait_recv()
+    lax.fori_loop(0, items + LAG * (line - 1) + BASE, step, 0)
+
     for e in range(examples):
         owner = (0 if e < examples // 2 else n_tensor - 2) + (e // each) % 2
 
@@ -195,7 +219,7 @@
     per = rank // n_tensor
     lane = lax.broadcasted_iota(jnp.int32, (examples, 2 * rank), 1)
     shift = me * per % group // per
-    total = None
+    columns = []
     for m in range(per // 2):
         picked = None
         for v in range(group // per):
@@ -203,11 +227,10 @@
             high = enc[:, v * per + 2 * m + 1, :]
             both = jnp.where(lane < rank, low, pltpu.roll(high, rank, 1))
             picked = both if picked is None else jnp.where(shift == v, both, picked)
-        rows = q_all[:, :, pl.ds(2 * rank * m, 2 * rank)].reshape(-1, 2 * rank)
-        add = lax.dot_general(picked, rows, (((1,), (1,)), ((), ())),
-                              precision=lax.Precision.HIGHEST, preferred_element_type=jnp.float32)
-        total = add if total is None else total + add
-    score[me] = total
+        columns.append(picked)
+    high, low = split(jnp.concatenate(columns, axis=1))
+    both = dot(jnp.concatenate([high, low], axis=0), q_high[...], (1, 1))
+    score[me] = both[:examples] + both[examples:] + dot(high, q_low[...], (1, 1))
 
     def score_copy(r):
         return pltpu.make_async_remote_copy(
@@ -266,31 +289,31 @@
     width = width_in + width_out
     group = max(rank // n_tensor, 8)
     f32, bf16, dma = jnp.float32, jnp.bfloat16, pltpu.SemaphoreType.DMA
-    anywhere = pl.BlockSpec(memory_space=pl.ANY)
+    in_hbm = pl.BlockSpec(memory_space=pltpu.HBM)
     tokens = examples * length
     return pl.pallas_call(
         functools.partial(kernel, n_dp, n_tensor),
         out_shape=jax.ShapeDtypeStruct((examples, n_query), f32),
-        in_specs=[anywhere] * 5,
+        in_specs=[in_hbm] * 5,
         out_specs=pl.BlockSpec(memory_space=pltpu.VMEM),
         scratch_shapes=[
             pltpu.VMEM((SLOTS, 4 * CHUNK, width), bf16), dma((SLOTS,)),
-            pltpu.VMEM((width_in, rank), bf16), pltpu.VMEM((width_out, rank), bf16),
-            pltpu.VMEM((width, 2 * rank), bf16), dma((2,)),
+            pltpu.VMEM((2 * rank, width), bf16), pltpu.VMEM((width, 2 * rank), bf16), dma((2,)),
             pltpu.VMEM((2, items, 2, CHUNK, 2 * rank), f32),
             pltpu.VMEM((2, items, CHUNK, 2 * rank), f32), dma((2, items)), dma((2, items)),
             pltpu.VMEM((2, items, CHUNK, 2 * rank), f32), dma((2, items)), dma((2, items)),
             pltpu.VMEM((examples // 4, 2 * rank, 2 * rank), f32),
             pltpu.VMEM((examples, group, 2 * rank), f32),
             dma((examples // 4, n_tensor - 1)), dma((examples,)),
-            pltpu.VMEM((n_dp,) + queries.shape, f32), dma(()), dma((n_dp - 1,)), dma((n_dp - 1,)),
+            pltpu.VMEM((n_dp,) + queries.shape, f32),
+            pltpu.VMEM((n_query, queries.shape[1]), bf16), pltpu.VMEM((n_query, queries.shape[1]), bf16), dma(()), dma((n_dp - 1,)), dma((n_dp - 1,)),
             pltpu.VMEM((n_tensor, examples, n_query), f32), dma((n_tensor - 1,)), dma((n_tensor - 1,)),
         ],
         compiler_params=pltpu.CompilerParams(
-            collective_id=0, has_side_effects=True, vmem_limit_bytes=48 * 1024 * 1024),
+            collective_id=0, has_side_effects=True, vmem_limit_bytes=63 * 1024 * 1024),
         cost_estimate=pl.CostEstimate(
             flops=2 * tokens * width * rank, bytes_accessed=2 * tokens * width, transcendentals=0),
-    )(acts, grads, proj_in, proj_out, queries)
+    )(acts, grads, proj_in.T, proj_out.T, queries)
 
 
 def solution(mesh):

time: 42.7 us -> 44.3 us (1.037)
  Pallas kernels: 38.4 us -> 42.8 us
  local copies, waits for them, and re-layouts: 4.02 us -> 1.3 us
    pallas_call x1, Pallas kernels: 38.4 us -> 42.8 us  [per_device(): pl.pallas_call(functools.partial(kernel, n_dp, n_tensor), out_shape=jax.S...]
    unnamed x5 -> x1, local copies, waits for them, and re-layouts: 4.02 us -> 1.3 us
where the time goes in v2:
time: 44.3 us; the launch traced here: 44.1 us
  Pallas kernels  42.8 us (97%)
  local copies, waits for them, and re-layouts  1.3 us (3%)
    pallas_call x1, Pallas kernels, per_device(): pl.pallas_call(functools.partial(kernel, n_dp, n_tensor), out_shape=jax.S...  42.8 us
    unnamed x1, local copies, waits for them, and re-layouts  1.3 us

profile of v2, /device:TPU:0, one launch (start us, length us, event | category | flops | bytes accessed | tf_op | source)
XLA Modules:
  0.0 44.1 jit_solution(12291836542444639494)
XLA Ops:
  0.0 42.8 %shard_map.55 = f32[8,256]{1,0:T(8,128)} custom-call(bf16[8,512,3584]{2,1,0:T(8,128)(2,1)} %acts.1, bf16[8,512,1024]{2,1,0:T(8,128)(2,1)} %grads.1, bf16[64,3584]{1,0:T(8,128)(2,1)} %bitcast.2, bf16[64,1024]{1,0:T(8,128)(2,1)} %bitcast.3, f32[64,512]{1,0:T(8,128)} %queries.1), custom_call_target="tpu_custom_call" | custom-call | flops 2415919104 | bytes 37748736 | tf_op jit(solution)/shard_map/pallas_call | solution.py:294
  42.8 1.3 %copy.7 = f32[8,256]{1,0:T(8,128)} copy(f32[8,256]{1,0:T(8,128)} %shard_map.55) | data formatting | bytes 16384

commit v3 on v2

--- a/solution.py
+++ b/solution.py
@@ -8,10 +8,10 @@
 from jax.sharding import PartitionSpec as P
 
 MESH = pl.DeviceIdType.MESH
-CHUNK = 64
-SLOTS = 5
-BASE = 2
-LAG = 3
+CHUNK = 128
+SLOTS = 4
+BASE = 1
+LAG = 2
 
 
 def split(value):
@@ -30,7 +30,7 @@
            q_all, q_high, q_low, q_own_sem, q_send, q_recv,
            score, score_send, score_recv):
     examples, length, width_in = acts.shape
-    width = x.shape[2]
+    width = x.shape[3]
     rank = proj_in.shape[0]
     blocks = length // CHUNK
     each = examples // 4
@@ -59,15 +59,13 @@
         for u in range(2):
             direction, item = where_is(s, u)
             start = pl.multiple_of((item % blocks) * CHUNK, CHUNK)
-            for owner in range(2):
-                e = (direction * 2 + owner) * each + item // blocks
-                rows = pl.ds((2 * u + owner) * CHUNK, CHUNK)
-                pltpu.make_async_copy(
-                    acts.at[e, pl.ds(start, CHUNK), :],
-                    x.at[slot, rows, pl.ds(0, width_in)], x_sem.at[slot]).start()
-                pltpu.make_async_copy(
-                    grads.at[e, pl.ds(start, CHUNK), :],
-                    x.at[slot, rows, pl.ds(width_in, width - width_in)], x_sem.at[slot]).start()
+            e = direction * 2 * each + 2 * (item // blocks)
+            pltpu.make_async_copy(
+                acts.at[pl.ds(e, 2), pl.ds(start, CHUNK), :],
+                x.at[slot, pl.ds(2 * u, 2), :, pl.ds(0, width_in)], x_sem.at[slot]).start()
+            pltpu.make_async_copy(
+                grads.at[pl.ds(e, 2), pl.ds(start, CHUNK), :],
+                x.at[slot, pl.ds(2 * u, 2), :, pl.ds(width_in, width - width_in)], x_sem.at[slot]).start()
 
     barrier = pltpu.get_barrier_semaphore()
     for r in range(1, n_tensor):
@@ -137,7 +135,7 @@
         def _():
             side = part[direction, item, core]
             j = item // blocks
-            e = (direction * 2 + core) * each + j
+            e = direction * 2 * each + 2 * j + core
             high, low = split(side)
             add = dot(jnp.concatenate([high, high, low], axis=0), jnp.concatenate([high, low, high], axis=0), (0, 0))
 
@@ -165,11 +163,14 @@
                 start_load(s + SLOTS - 1)
 
             pltpu.make_async_copy(x.at[slot], x.at[slot], x_sem.at[slot]).wait()
-            sides = jnp.dot(x[slot], w[...], preferred_element_type=jnp.float32)
+            halves = []
+            for h in range(2):
+                lanes = pl.ds(h * (width // 2), width // 2)
+                halves.append(dot(x[slot, :, :, lanes].reshape(4 * CHUNK, width // 2), w[lanes, :], (1, 0)))
+            sides = halves[0] + halves[1]
             for u in range(2):
                 direction, item = where_is(s, u)
-                for owner in range(2):
-                    part[direction, item, owner] = sides[(2 * u + owner) * CHUNK:(2 * u + owner + 1) * CHUNK]
+                part[direction, item] = sides[2 * u * CHUNK:2 * (u + 1) * CHUNK].reshape(2, CHUNK, 2 * rank)
 
             @pl.when(s == 0)
             def _():
@@ -210,7 +211,7 @@
     lax.fori_loop(0, items + LAG * (line - 1) + BASE, step, 0)
 
     for e in range(examples):
-        owner = (0 if e < examples // 2 else n_tensor - 2) + (e // each) % 2
+        owner = (0 if e < examples // 2 else n_tensor - 2) + e % 2
 
         @pl.when(me != owner)
         def _():
@@ -297,7 +298,7 @@
         in_specs=[in_hbm] * 5,
         out_specs=pl.BlockSpec(memory_space=pltpu.VMEM),
         scratch_shapes=[
-            pltpu.VMEM((SLOTS, 4 * CHUNK, width), bf16), dma((SLOTS,)),
+            pltpu.VMEM((SLOTS, 4, CHUNK, width), bf16), dma((SLOTS,)),
             pltpu.VMEM((2 * rank, width), bf16), pltpu.VMEM((width, 2 * rank), bf16), dma((2,)),
             pltpu.VMEM((2, items, 2, CHUNK, 2 * rank), f32),
             pltpu.VMEM((2, items, CHUNK, 2 * rank), f32), dma((2, items)), dma((2, items)),

time: 44.3 us -> 40.1 us (0.905)
  Pallas kernels: 42.8 us -> 38.6 us
    pallas_call x1, Pallas kernels: 42.8 us -> 38.6 us  [per_device(): pl.pallas_call(functools.partial(kernel, n_dp, n_tensor), out_shape=jax.S...]
where the time goes in v3:
time: 40.1 us; the launch traced here: 39.9 us
  Pallas kernels  38.6 us (96%)
  local copies, waits for them, and re-layouts  1.3 us (3%)
    pallas_call x1, Pallas kernels, per_device(): pl.pallas_call(functools.partial(kernel, n_dp, n_tensor), out_shape=jax.S...  38.6 us
    unnamed x1, local copies, waits for them, and re-layouts  1.3 us

profile of v3, /device:TPU:0, one launch (start us, length us, event | category | flops | bytes accessed | tf_op | source)
XLA Modules:
  0.0 39.9 jit_solution(8118574203590070894)
XLA Ops:
  0.0 38.6 %shard_map.55 = f32[8,256]{1,0:T(8,128)} custom-call(bf16[8,512,3584]{2,1,0:T(8,128)(2,1)} %acts.1, bf16[8,512,1024]{2,1,0:T(8,128)(2,1)} %grads.1, bf16[64,3584]{1,0:T(8,128)(2,1)} %bitcast.2, bf16[64,1024]{1,0:T(8,128)(2,1)} %bitcast.3, f32[64,512]{1,0:T(8,128)} %queries.1), custom_call_target="tpu_custom_call" | custom-call | flops 2415919104 | bytes 37748736 | tf_op jit(solution)/shard_map/pallas_call | solution.py:295
  38.6 1.3 %copy.7 = f32[8,256]{1,0:T(8,128)} copy(f32[8,256]{1,0:T(8,128)} %shard_map.55) | data formatting | bytes 16384

commit v4 on v3

--- a/solution.py
+++ b/solution.py
@@ -9,9 +9,9 @@
 
 MESH = pl.DeviceIdType.MESH
 CHUNK = 128
-SLOTS = 4
+SLOTS = 3
 BASE = 1
-LAG = 2
+EXTRA = 2
 
 
 def split(value):
@@ -62,10 +62,10 @@
             e = direction * 2 * each + 2 * (item // blocks)
             pltpu.make_async_copy(
                 acts.at[pl.ds(e, 2), pl.ds(start, CHUNK), :],
-                x.at[slot, pl.ds(2 * u, 2), :, pl.ds(0, width_in)], x_sem.at[slot]).start()
+                x.at[slot, pl.ds(2 * u, 2), :, pl.ds(0, width_in)], x_sem.at[slot]).start(priority=1)
             pltpu.make_async_copy(
                 grads.at[pl.ds(e, 2), pl.ds(start, CHUNK), :],
-                x.at[slot, pl.ds(2 * u, 2), :, pl.ds(width_in, width - width_in)], x_sem.at[slot]).start()
+                x.at[slot, pl.ds(2 * u, 2), :, pl.ds(width_in, width - width_in)], x_sem.at[slot]).start(priority=1)
 
     barrier = pltpu.get_barrier_semaphore()
     for r in range(1, n_tensor):
@@ -118,6 +118,9 @@
             send_sem=enc_send.at[j, r - 1], recv_sem=enc_recv.at[e],
             device_id={"tensor": to}, device_id_type=MESH)
 
+    def lag(hops):
+        return BASE + hops + jnp.where(hops >= line // 2, EXTRA, 0)
+
     def process(direction, item, hops):
         pair_copy(direction, item).wait_recv()
         part[direction, item, core] = part[direction, item, core] + pair[direction, item]
@@ -191,7 +194,7 @@
             q_high[...] = high
             q_low[...] = low
 
-        first = jnp.where(is_end, 2 * (s - BASE), s - BASE - LAG * near_hops)
+        first = jnp.where(is_end, 2 * (s - BASE), s - lag(near_hops))
         count = jnp.where(is_end, 2, 1)
         for u in range(2):
             item = first + u
@@ -200,7 +203,7 @@
             def _():
                 process(near, item, near_hops)
 
-        item_far = s - BASE - LAG * far_hops
+        item_far = s - lag(far_hops)
 
         @pl.when(jnp.logical_and(item_far >= 0, item_far < items))
         def _():
@@ -208,7 +211,7 @@
 
         return carry
 
-    lax.fori_loop(0, items + LAG * (line - 1) + BASE, step, 0)
+    lax.fori_loop(0, items + BASE + line - 1 + EXTRA, step, 0)
 
     for e in range(examples):
         owner = (0 if e < examples // 2 else n_tensor - 2) + e % 2

time: 40.1 us -> 40.1 us (level)
  no operation moved by 1% of the time
where the time goes in v4:
time: 40.1 us; the launch traced here: 39.9 us
  Pallas kernels  38.6 us (96%)
  local copies, waits for them, and re-layouts  1.3 us (3%)
    pallas_call x1, Pallas kernels, per_device(): pl.pallas_call(functools.partial(kernel, n_dp, n_tensor), out_shape=jax.S...  38.6 us
    unnamed x1, local copies, waits for them, and re-layouts  1.3 us

profile of v4, /device:TPU:0, one launch (start us, length us, event | category | flops | bytes accessed | tf_op | source)
XLA Modules:
  0.0 39.9 jit_solution(3916543768943153634)
XLA Ops:
  0.0 38.6 %shard_map.55 = f32[8,256]{1,0:T(8,128)} custom-call(bf16[8,512,3584]{2,1,0:T(8,128)(2,1)} %acts.1, bf16[8,512,1024]{2,1,0:T(8,128)(2,1)} %grads.1, bf16[64,3584]{1,0:T(8,128)(2,1)} %bitcast.2, bf16[64,1024]{1,0:T(8,128)(2,1)} %bitcast.3, f32[64,512]{1,0:T(8,128)} %queries.1), custom_call_target="tpu_custom_call" | custom-call | flops 2415919104 | bytes 37748736 | tf_op jit(solution)/shard_map/pallas_call | solution.py:298
  38.6 1.3 %copy.7 = f32[8,256]{1,0:T(8,128)} copy(f32[8,256]{1,0:T(8,128)} %shard_map.55) | data formatting | bytes 16384

commit v5 on v4

--- a/solution.py
+++ b/solution.py
@@ -24,7 +24,7 @@
 
 
 def kernel(n_dp, n_tensor, acts, grads, proj_in, proj_out, queries, out,
-           x, x_sem, w_side, w, w_sem,
+           x, x_sem, w_in, w_out, w_sem,
            part, pair, pair_send, pair_recv, chain, chain_send, chain_recv,
            gram, enc, enc_send, enc_recv,
            q_all, q_high, q_low, q_own_sem, q_send, q_recv,
@@ -73,21 +73,16 @@
     for r in range(1, n_dp):
         pl.semaphore_signal(barrier, inc=1, device_id={"dp": (me_dp + r) % n_dp}, device_id_type=MESH)
 
-    in_lanes, out_lanes = pl.ds(0, width_in), pl.ds(width_in, width - width_in)
-    in_rows, out_rows = pl.ds(0, rank), pl.ds(rank, rank)
-    load_in = pltpu.make_async_copy(proj_in, w_side.at[in_rows, in_lanes], w_sem.at[0])
-    load_out = pltpu.make_async_copy(proj_out, w_side.at[out_rows, out_lanes], w_sem.at[1])
+    load_in = pltpu.make_async_copy(proj_in, w_in, w_sem.at[0])
+    load_out = pltpu.make_async_copy(proj_out, w_out, w_sem.at[1])
     load_in.start()
     load_out.start()
     for s in range(SLOTS - 1):
         start_load(s)
     q_own = pltpu.make_async_copy(queries, q_all.at[me_dp], q_own_sem)
     q_own.start()
-    w_side[out_rows, in_lanes] = jnp.zeros((rank, width_in), w_side.dtype)
-    w_side[in_rows, out_lanes] = jnp.zeros((rank, width - width_in), w_side.dtype)
     load_in.wait()
     load_out.wait()
-    w[...] = w_side[...].T
 
     def query_copy(r):
         return pltpu.make_async_remote_copy(
@@ -140,7 +135,7 @@
             j = item // blocks
             e = direction * 2 * each + 2 * j + core
             high, low = split(side)
-            add = dot(jnp.concatenate([high, high, low], axis=0), jnp.concatenate([high, low, high], axis=0), (0, 0))
+            add = dot(jnp.concatenate([high, high, low], axis=1), jnp.concatenate([high, low, high], axis=1), (1, 1))
 
             @pl.when(item % blocks == 0)
             def _():
@@ -166,14 +161,16 @@
                 start_load(s + SLOTS - 1)
 
             pltpu.make_async_copy(x.at[slot], x.at[slot], x_sem.at[slot]).wait()
-            halves = []
-            for h in range(2):
-                lanes = pl.ds(h * (width // 2), width // 2)
-                halves.append(dot(x[slot, :, :, lanes].reshape(4 * CHUNK, width // 2), w[lanes, :], (1, 0)))
-            sides = halves[0] + halves[1]
+            tokens_in = x[slot, :, :, pl.ds(0, width_in)].reshape(4 * CHUNK, width_in)
+            tokens_out = x[slot, :, :, pl.ds(width_in, width - width_in)].reshape(4 * CHUNK, width - width_in)
+            sides_in = dot(w_in[...], tokens_in, (1, 1))
+            sides_out = dot(w_out[...], tokens_out, (1, 1))
             for u in range(2):
                 direction, item = where_is(s, u)
-                part[direction, item] = sides[2 * u * CHUNK:2 * (u + 1) * CHUNK].reshape(2, CHUNK, 2 * rank)
+                for owner in range(2):
+                    lanes = slice((2 * u + owner) * CHUNK, (2 * u + owner + 1) * CHUNK)
+                    part[direction, item, owner, pl.ds(0, rank), :] = sides_in[:, lanes]
+                    part[direction, item, owner, pl.ds(rank, rank), :] = sides_out[:, lanes]
 
             @pl.when(s == 0)
             def _():
@@ -302,10 +299,10 @@
         out_specs=pl.BlockSpec(memory_space=pltpu.VMEM),
         scratch_shapes=[
             pltpu.VMEM((SLOTS, 4, CHUNK, width), bf16), dma((SLOTS,)),
-            pltpu.VMEM((2 * rank, width), bf16), pltpu.VMEM((width, 2 * rank), bf16), dma((2,)),
-            pltpu.VMEM((2, items, 2, CHUNK, 2 * rank), f32),
-            pltpu.VMEM((2, items, CHUNK, 2 * rank), f32), dma((2, items)), dma((2, items)),
-            pltpu.VMEM((2, items, CHUNK, 2 * rank), f32), dma((2, items)), dma((2, items)),
+            pltpu.VMEM((rank, width_in), bf16), pltpu.VMEM((rank, width_out), bf16), dma((2,)),
+            pltpu.VMEM((2, items, 2, 2 * rank, CHUNK), f32),
+            pltpu.VMEM((2, items, 2 * rank, CHUNK), f32), dma((2, items)), dma((2, items)),
+            pltpu.VMEM((2, items, 2 * rank, CHUNK), f32), dma((2, items)), dma((2, items)),
             pltpu.VMEM((examples // 4, 2 * rank, 2 * rank), f32),
             pltpu.VMEM((examples, group, 2 * rank), f32),
             dma((examples // 4, n_tensor - 1)), dma((examples,)),

time: 40.1 us -> 41.2 us (1.027)
  Pallas kernels: 38.6 us -> 39.7 us
    pallas_call x1, Pallas kernels: 38.6 us -> 39.7 us  [per_device(): pl.pallas_call(functools.partial(kernel, n_dp, n_tensor), out_shape=jax.S...]
where the time goes in v5:
time: 41.2 us; the launch traced here: 41 us
  Pallas kernels  39.7 us (96%)
  local copies, waits for them, and re-layouts  1.3 us (3%)
    pallas_call x1, Pallas kernels, per_device(): pl.pallas_call(functools.partial(kernel, n_dp, n_tensor), out_shape=jax.S...  39.7 us
    unnamed x1, local copies, waits for them, and re-layouts  1.3 us

profile of v5, /device:TPU:0, one launch (start us, length us, event | category | flops | bytes accessed | tf_op | source)
XLA Modules:
  0.0 41.0 jit_solution(17969791476381843723)
XLA Ops:
  0.0 39.7 %shard_map.55 = f32[8,256]{1,0:T(8,128)} custom-call(bf16[8,512,3584]{2,1,0:T(8,128)(2,1)} %acts.1, bf16[8,512,1024]{2,1,0:T(8,128)(2,1)} %grads.1, bf16[64,3584]{1,0:T(8,128)(2,1)} %bitcast.2, bf16[64,1024]{1,0:T(8,128)(2,1)} %bitcast.3, f32[64,512]{1,0:T(8,128)} %queries.1), custom_call_target="tpu_custom_call" | custom-call | flops 2415919104 | bytes 37748736 | tf_op jit(solution)/shard_map/pallas_call | solution.py:295
  39.7 1.3 %copy.7 = f32[8,256]{1,0:T(8,128)} copy(f32[8,256]{1,0:T(8,128)} %shard_map.55) | data formatting | bytes 16384

commit v6 on v4

--- a/solution.py
+++ b/solution.py
@@ -11,7 +11,7 @@
 CHUNK = 128
 SLOTS = 3
 BASE = 1
-EXTRA = 2
+EXTRA = 1
 
 
 def split(value):
@@ -50,8 +50,15 @@
     def where_is(s, u):
         half = items // 2
         late = s // half
-        direction = jnp.where(is_end, near + late - 2 * near * late, u)
-        item = jnp.where(is_end, 2 * (s % half) + u, s)
+        first, last = s == 0, s == items - 1
+        if u == 0:
+            between = jnp.where(last, 1 - near, near)
+            item = jnp.where(first, 0, jnp.where(last, items - 2, s + 1))
+        else:
+            between = jnp.where(first, near, 1 - near)
+            item = jnp.where(first, 1, jnp.where(last, items - 1, s - 1))
+        direction = jnp.where(is_end, near + late - 2 * near * late, between)
+        item = jnp.where(is_end, 2 * (s % half) + u, item)
         return direction, item
 
     def start_load(s):
@@ -112,14 +119,13 @@
         return pl.ds(pl.multiple_of((rank + t * rank // n_tensor) // group * group, group), group)
 
     def enc_copy(j, e, r):
-        to = (me + r) % n_tensor
+        to = (me + jnp.where(place < line // 2, r, n_tensor - r)) % n_tensor
         return pltpu.make_async_remote_copy(
             src_ref=gram.at[j, enc_rows(to), :], dst_ref=enc.at[e],
             send_sem=enc_send.at[j, r - 1], recv_sem=enc_recv.at[e],
             device_id={"tensor": to}, device_id_type=MESH)
 
-    def lag(hops):
-        return BASE + hops + jnp.where(hops >= line // 2, EXTRA, 0)
+    far_lag = jnp.where(is_end, max(line - 1 + EXTRA, items // 2 + BASE), far_hops + EXTRA)
 
     def process(direction, item, hops):
         pair_copy(direction, item).wait_recv()
@@ -152,7 +158,7 @@
 
             @pl.when(item % blocks == blocks - 1)
             def _():
-                for r in range(1, n_tensor):
+                for r in range(n_tensor - 1, 0, -1):
                     enc_copy(j, e, r).start()
                 enc[e] = gram[j, enc_rows(me), :]
 
@@ -166,11 +172,7 @@
                 start_load(s + SLOTS - 1)
 
             pltpu.make_async_copy(x.at[slot], x.at[slot], x_sem.at[slot]).wait()
-            halves = []
-            for h in range(2):
-                lanes = pl.ds(h * (width // 2), width // 2)
-                halves.append(dot(x[slot, :, :, lanes].reshape(4 * CHUNK, width // 2), w[lanes, :], (1, 0)))
-            sides = halves[0] + halves[1]
+            sides = dot(x[slot].reshape(4 * CHUNK, width), w[...], (1, 0))
             for u in range(2):
                 direction, item = where_is(s, u)
                 part[direction, item] = sides[2 * u * CHUNK:2 * (u + 1) * CHUNK].reshape(2, CHUNK, 2 * rank)
@@ -194,8 +196,9 @@
             q_high[...] = high
             q_low[...] = low
 
-        first = jnp.where(is_end, 2 * (s - BASE), s - lag(near_hops))
-        count = jnp.where(is_end, 2, 1)
+        opening = s == near_hops + BASE
+        first = jnp.where(is_end, 2 * (s - BASE), jnp.where(opening, 0, s - near_hops))
+        count = jnp.where(jnp.logical_or(is_end, opening), 2, jnp.where(s > near_hops + BASE, 1, 0))
         for u in range(2):
             item = first + u
 
@@ -203,7 +206,7 @@
             def _():
                 process(near, item, near_hops)
 
-        item_far = s - lag(far_hops)
+        item_far = s - far_lag
 
         @pl.when(jnp.logical_and(item_far >= 0, item_far < items))
         def _():
@@ -211,7 +214,7 @@
 
         return carry
 
-    lax.fori_loop(0, items + BASE + line - 1 + EXTRA, step, 0)
+    lax.fori_loop(0, items + max(line - 1 + EXTRA, items // 2 + BASE), step, 0)
 
     for e in range(examples):
         owner = (0 if e < examples // 2 else n_tensor - 2) + e % 2

time: 40.1 us -> 40.6 us (1.012)
    pallas_call x1, Pallas kernels: 38.6 us -> 39 us  [per_device(): pl.pallas_call(functools.partial(kernel, n_dp, n_tensor), out_shape=jax.S...]
where the time goes in v6:
time: 40.6 us; the launch traced here: 40.3 us
  Pallas kernels  39 us (96%)
  local copies, waits for them, and re-layouts  1.3 us (3%)
    pallas_call x1, Pallas kernels, per_device(): pl.pallas_call(functools.partial(kernel, n_dp, n_tensor), out_shape=jax.S...  39 us
    unnamed x1, local copies, waits for them, and re-layouts  1.3 us

profile of v6, /device:TPU:0, one launch (start us, length us, event | category | flops | bytes accessed | tf_op | source)
XLA Modules:
  0.0 40.3 jit_solution(3129114743016395194)
XLA Ops:
  0.0 39.0 %shard_map.55 = f32[8,256]{1,0:T(8,128)} custom-call(bf16[8,512,3584]{2,1,0:T(8,128)(2,1)} %acts.1, bf16[8,512,1024]{2,1,0:T(8,128)(2,1)} %grads.1, bf16[64,3584]{1,0:T(8,128)(2,1)} %bitcast.2, bf16[64,1024]{1,0:T(8,128)(2,1)} %bitcast.3, f32[64,512]{1,0:T(8,128)} %queries.1), custom_call_target="tpu_custom_call" | custom-call | flops 2415919104 | bytes 37748736 | tf_op jit(solution)/shard_map/pallas_call | solution.py:301
  39.0 1.3 %copy.7 = f32[8,256]{1,0:T(8,128)} copy(f32[8,256]{1,0:T(8,128)} %shard_map.55) | data formatting | bytes 16384
